TPU v7x, 128 devices: a whole 4x4x4 slice. The times are simulated.
128 devices in a mesh: spec: 16 (over y_lo, x, core), wave: 8 (over z, y_hi).
Axes of the slice: x: 4, y: 4 (y_hi: 2, y_lo: 2; y = y_hi * 2 + y_lo), z: 4, core: 2. Of those that a mesh axis runs over, the one named last changes fastest.
Arguments:
- spectra: bfloat16 [16384, 7168], P('spec', 'wave'), may hold values from 0.049804688 to 5
- offsets: int32 [64], P('spec'), may hold values from 0 to 7167, as said below
- cover_lo: int32 [16384], P('spec'), may hold values from 0 to 7167, as said below
- cover_hi: int32 [16384], P('spec'), may hold values from 5377 to 7168
- coefficients: float32 [16384, 128], P('spec'), may hold values from 0.03 to 0.3
- templates: float32 [128, 7168], P(None, 'wave'), may hold values from 0.03 to 0.3
Outputs:
- templates_new: float32 [128, 7168], P(None, 'wave')
- coefficients_new: float32 [16384, 128], P('spec')
Inputs may be any that keep to these rules, and one draw needn't show every extreme that they name: `offsets`: the first block of each index of spec has an offset of at least 6272; the last block's offset is 7167. cover_lo < cover_hi for every spectrum; about one spectrum in eight has weight one only on its last 1 to 4 observed pixels, cover_hi = 7168; the others have cover_lo < 1792 and cover_hi > 5376.
All inputs are finite; a program needn't handle non-finite values.
Results may differ from a plain program's by a relative error of at most 0.0012.
Values may be sent and summed in bfloat16 or wider, within the bound.
No kernel may reach another device: no remote copies, remote signals or barrier semaphores. Data moves between devices by JAX's collectives and lax.ppermute only.
A program may use at most 128 MiB of HBM per device.

v0:
```python
import jax
import jax.numpy as jnp
from jax import lax
from jax.sharding import PartitionSpec as P

ITERS = 4


def take_blocks(joined, starts, blocks, width):
    rows = joined.shape[0]
    grouped = joined.reshape(blocks, rows // blocks, joined.shape[1])
    picked = jax.vmap(lambda piece, start: lax.dynamic_slice_in_dim(piece, start, width, 1))(
        grouped, starts
    )
    return picked.reshape(rows, width)


def ratio_of(rest, weight, coef_bf, temps_bf):
    model = jnp.dot(coef_bf, temps_bf, preferred_element_type=jnp.float32)
    inside = weight > 0
    return jnp.where(inside, rest.astype(jnp.float32) / jnp.where(inside, model, 1.0), 0.0).astype(
        jnp.bfloat16
    )


def over_rows(left, right):
    return lax.dot_general(
        left, right, (((0,), (0,)), ((), ())), preferred_element_type=jnp.float32
    )


def over_pixels(left, right):
    return lax.dot_general(
        left, right, (((1,), (1,)), ((), ())), preferred_element_type=jnp.float32
    )


def template_update(temps, num_t, den_t):
    num_a, den_a = lax.psum((num_t, den_t), "spec")
    return temps * num_a / jnp.maximum(den_a, 1.0)


def coef_update(coef, num_c, den_c):
    num_a, den_a = lax.psum((num_c, den_c), "wave")
    return coef * num_a / jnp.maximum(den_a, 1.0)


def shards(spectra, offsets, cover_lo, cover_hi, coefficients, templates):
    rows, width = spectra.shape
    blocks = offsets.shape[0]
    block_rows = rows // blocks
    wave_pos = lax.axis_index("wave")
    row_off = jnp.repeat(offsets, block_rows)
    whole = lax.all_gather(spectra, "wave", axis=1, tiled=True)
    joined = jnp.concatenate([whole, jnp.zeros((rows, width), whole.dtype)], axis=1)
    starts = jnp.minimum(wave_pos * width + offsets, whole.shape[1])
    rest = take_blocks(joined, starts, blocks, width)
    pixel = wave_pos * width + jnp.arange(width, dtype=jnp.int32)
    observed = pixel[None, :] + row_off[:, None]
    weight = ((observed >= cover_lo[:, None]) & (observed < cover_hi[:, None])).astype(jnp.bfloat16)
    temps = templates
    coef = coefficients
    for update in range(ITERS):
        coef_bf = coef.astype(jnp.bfloat16)
        ratio = ratio_of(rest, weight, coef_bf, temps.astype(jnp.bfloat16))
        temps = template_update(temps, over_rows(coef_bf, ratio), over_rows(coef_bf, weight))
        temps_bf = temps.astype(jnp.bfloat16)
        ratio_new = ratio_of(rest, weight, coef_bf, temps_bf)
        coef = coef_update(coef, over_pixels(ratio_new, temps_bf), over_pixels(weight, temps_bf))
    return (temps, coef)


def solution(mesh):
    in_specs = (
        P("spec", "wave"),
        P("spec"),
        P("spec"),
        P("spec"),
        P("spec", None),
        P(None, "wave"),
    )
    out_specs = (P(None, "wave"), P("spec", None))
    return jax.shard_map(shards, mesh=mesh, in_specs=in_specs, out_specs=out_specs, check_vma=False)
```

profile of v0, /device:TPU:0, one launch (start us, length us, event | category | flops | bytes accessed | tf_op | source)
XLA Modules:
  0.0 1094.3 jit_solution(7808599163899580070)
XLA Ops:
  7.2 0.0 all-gather.2.cloned.1.call-start
  7.2 0.7 all-gather.2.cloned.1.call-update
  7.9 0.0 all-reduce.25.cloned.1.call-start
  8.0 0.7 broadcast_bitcast_fusion
  8.7 0.7 fusion.32
  9.4 0.1 copy.8
  9.5 3.4 convolution_bitcast_fusion
  12.9 163.0 %all-gather.2.cloned.1.call-done = bf16[1024,7168]{1,0:T(8,128)(2,1)} async-done(((bf16[1024,896]{1,0:T(8,128)(2,1)}), bf16[1024,7168]{1,0:T(8,128)(2,1)}) %all-gather.2.cloned.1.call-update) | async-done | bytes 14680080 | tf_op jit(solution)/shard_map/all_gather | solution.py:54
  175.9 12.9 %concatenate.6 = bf16[1024,8064]{1,0:T(8,128)(2,1)} pad(bf16[1024,7168]{1,0:T(8,128)(2,1)} %all-gather.2.cloned.1.call-done, bf16[]{:T(256)} %constant.10.clone.1), padding=0_0x0_896 | pad | bytes 31195138 | tf_op jit(solution)/shard_map/concatenate | solution.py:55
  188.8 12.5 %while.1 = (s32[]{:T(128)}, bf16[4,256,8064]{2,1,0:T(8,128)(2,1)}, s32[4,3]{1,0:T(4,128)S(1)}, bf16[4,256,896]{2,1,0:T(8,128)(2,1)S(1)}, s32[]{:T(128)}) while((s32[]{:T(128)}, bf16[4,256,8064]{2,1,0:T(8,128)(2,1)}, s32[4,3]{1,0:T(4,128)S(1)}, bf16[4,256,896]{2,1,0:T(8,128)(2,1)S(1)}, s32[]{:T(128)}) %tuple.54), condition=%wide.while_cond, body=%wide.while_body.sunk | while | flops 2 | bytes 917621 | solution.py:12
  188.8 0.6 fusion.108
  189.4 2.5 dynamic-slice_dynamic-update-slice_fusion.2
  191.9 0.6 fusion.108
  192.5 2.5 dynamic-slice_dynamic-update-slice_fusion.2
  195.1 0.6 fusion.108
  195.7 2.5 dynamic-slice_dynamic-update-slice_fusion.2
  198.2 0.6 fusion.108
  198.8 2.5 dynamic-slice_dynamic-update-slice_fusion.2
  201.4 2.9 fusion.25
  204.3 0.0 all-reduce.25.cloned.1.call-update
  204.3 0.0 all-reduce.33.cloned.1.call-start
  204.3 0.2 copy.9
  204.5 116.8 %all-reduce.25.cloned.1.call-done = (f32[128,896]{0,1:T(8,128)}, f32[128,896]{0,1:T(8,128)}) async-done(((f32[128,896]{0,1:T(8,128)}, f32[128,896]{0,1:T(8,128)}), (f32[128,896]{0,1:T(8,128)}, f32[128,896]{0,1:T(8,128)})) %all-reduce.25.cloned.1.call-update) | async-done | bytes 917520 | tf_op jit(solution)/shard_map/psum | solution.py:39
  321.3 1.2 maximum_divide_fusion.7
  322.5 2.5 fusion.20
  325.1 2.0 fusion.63
  327.0 0.0 all-reduce.33.cloned.1.call-update
  327.1 0.0 all-reduce.23.cloned.1.call-start
  327.1 92.3 %all-reduce.33.cloned.1.call-done = (f32[1024,128]{1,0:T(8,128)}, f32[1024,128]{1,0:T(8,128)}) async-done(((f32[1024,128]{1,0:T(8,128)}, f32[1024,128]{1,0:T(8,128)}), (f32[1024,128]{1,0:T(8,128)}, f32[1024,128]{1,0:T(8,128)})) %all-reduce.33.cloned.1.call-update) | async-done | bytes 1048592 | tf_op jit(solution)/shard_map/psum | solution.py:44
  419.4 1.3 maximum_divide_fusion.3
  420.7 3.2 fusion.24
  423.9 2.4 fusion.57
  426.2 0.0 all-reduce.23.cloned.1.call-update
  426.3 0.2 all-reduce.31.cloned.1.call-start
  426.5 117.0 %all-reduce.23.cloned.1.call-done = (f32[128,896]{0,1:T(8,128)}, f32[128,896]{0,1:T(8,128)}) async-done(((f32[128,896]{0,1:T(8,128)}, f32[128,896]{0,1:T(8,128)}), (f32[128,896]{0,1:T(8,128)}, f32[128,896]{0,1:T(8,128)})) %all-reduce.23.cloned.1.call-update) | async-done | bytes 917520 | tf_op jit(solution)/shard_map/psum | solution.py:39
  543.5 1.2 maximum_divide_fusion.6
  544.7 2.5 fusion.19
  547.3 2.0 fusion.51
  549.2 0.0 all-reduce.31.cloned.1.call-update
  549.2 0.0 all-reduce.21.cloned.1.call-start
  549.3 92.2 %all-reduce.31.cloned.1.call-done = (f32[1024,128]{1,0:T(8,128)}, f32[1024,128]{1,0:T(8,128)}) async-done(((f32[1024,128]{1,0:T(8,128)}, f32[1024,128]{1,0:T(8,128)}), (f32[1024,128]{1,0:T(8,128)}, f32[1024,128]{1,0:T(8,128)})) %all-reduce.31.cloned.1.call-update) | async-done | bytes 1048592 | tf_op jit(solution)/shard_map/psum | solution.py:44
  641.5 1.3 maximum_divide_fusion.2
  642.8 3.2 fusion.23
  646.0 2.4 fusion.45
  648.3 0.0 all-reduce.21.cloned.1.call-update
  648.4 0.0 all-reduce.29.cloned.1.call-start
  648.4 117.2 %all-reduce.21.cloned.1.call-done = (f32[128,896]{0,1:T(8,128)}, f32[128,896]{0,1:T(8,128)}) async-done(((f32[128,896]{0,1:T(8,128)}, f32[128,896]{0,1:T(8,128)}), (f32[128,896]{0,1:T(8,128)}, f32[128,896]{0,1:T(8,128)})) %all-reduce.21.cloned.1.call-update) | async-done | bytes 917520 | tf_op jit(solution)/shard_map/psum | solution.py:39
  765.6 1.2 maximum_divide_fusion.5
  766.8 2.5 fusion.18
  769.3 2.0 fusion.39
  771.3 0.0 all-reduce.29.cloned.1.call-update
  771.3 0.3 all-reduce.19.cloned.1.call-start
  771.6 92.0 %all-reduce.29.cloned.1.call-done = (f32[1024,128]{1,0:T(8,128)}, f32[1024,128]{1,0:T(8,128)}) async-done(((f32[1024,128]{1,0:T(8,128)}, f32[1024,128]{1,0:T(8,128)}), (f32[1024,128]{1,0:T(8,128)}, f32[1024,128]{1,0:T(8,128)})) %all-reduce.29.cloned.1.call-update) | async-done | bytes 1048592 | tf_op jit(solution)/shard_map/psum | solution.py:44
  863.6 1.3 maximum_divide_fusion.1
  864.9 3.2 fusion.22
  868.1 2.4 fusion.33
  870.5 0.0 all-reduce.27.cloned.1.call-start
  870.5 117.2 %all-reduce.19.cloned.1.call-done = (f32[128,896]{0,1:T(8,128)}, f32[128,896]{0,1:T(8,128)}) async-done(((f32[128,896]{0,1:T(8,128)}, f32[128,896]{0,1:T(8,128)}), (f32[128,896]{0,1:T(8,128)}, f32[128,896]{0,1:T(8,128)})) %all-reduce.19.cloned.1.call-update) | async-done | bytes 917520 | tf_op jit(solution)/shard_map/psum | solution.py:39
  987.7 1.2 maximum_divide_fusion.4
  988.9 2.5 fusion.17
  991.5 2.0 fusion.30
  993.4 1.0 copy.16
  994.4 91.3 %all-reduce.27.cloned.1.call-done = (f32[1024,128]{1,0:T(8,128)}, f32[1024,128]{1,0:T(8,128)}) async-done(((f32[1024,128]{1,0:T(8,128)}, f32[1024,128]{1,0:T(8,128)}), (f32[1024,128]{1,0:T(8,128)}, f32[1024,128]{1,0:T(8,128)})) %all-reduce.27.cloned.1.call-update) | async-done | bytes 1048592 | tf_op jit(solution)/shard_map/psum | solution.py:44
  1085.7 2.1 maximum_divide_fusion
  (19 shorter events, 0.1 us)
Async XLA Ops:
  7.2 168.7 %all-gather.2.cloned.1.call-start = ((), (), s32[]{:S(2)}) async-start(), calls=%async_computation | async-start | bytes 16515072 | tf_op jit(solution)/shard_map/all_gather | solution.py:54
  7.9 313.4 %all-reduce.25.cloned.1.call-start = ((), (), s32[]{:S(2)}) async-start(), calls=%async_computation.4 | async-start | bytes 1835008 | tf_op jit(solution)/shard_map/psum | solution.py:39
  175.9 25.5 %copy-start.1 = (f32[128,896]{1,0:T(8,128)S(1)}, f32[128,896]{1,0:T(8,128)}, u32[]{:S(2)}) copy-start(f32[128,896]{1,0:T(8,128)} %param.11) | copy-start | bytes 1376260
  188.8 12.6 %copy-start = (f32[1024,128]{1,0:T(8,128)S(1)}, f32[1024,128]{1,0:T(8,128)}, u32[]{:S(2)}) copy-start(f32[1024,128]{1,0:T(8,128)} %param.10) | copy-start | bytes 1572868
  188.8 12.6 %copy-start.2 = (s32[1024]{0:T(1024)S(1)}, s32[1024]{0:T(1024)}, u32[]{:S(2)}) copy-start(s32[1024]{0:T(1024)} %param.9) | copy-start | bytes 12292
  188.8 12.6 %copy-start.3 = (s32[1024]{0:T(1024)S(1)}, s32[1024]{0:T(1024)}, u32[]{:S(2)}) copy-start(s32[1024]{0:T(1024)} %param.8) | copy-start | bytes 12292
  204.3 215.1 %all-reduce.33.cloned.1.call-start = ((), (), s32[]{:S(2)}) async-start(), calls=%async_computation.8 | async-start | bytes 2097152 | tf_op jit(solution)/shard_map/psum | solution.py:44
  327.1 216.4 %all-reduce.23.cloned.1.call-start = ((), (), s32[]{:S(2)}) async-start(), calls=%async_computation.3 | async-start | bytes 1835008 | tf_op jit(solution)/shard_map/psum | solution.py:39
  426.3 215.2 %all-reduce.31.cloned.1.call-start = ((), (), s32[]{:S(2)}) async-start(), calls=%async_computation.7 | async-start | bytes 2097152 | tf_op jit(solution)/shard_map/psum | solution.py:44
  549.2 216.3 %all-reduce.21.cloned.1.call-start = ((), (), s32[]{:S(2)}) async-start(), calls=%async_computation.2 | async-start | bytes 1835008 | tf_op jit(solution)/shard_map/psum | solution.py:39
  648.4 215.2 %all-reduce.29.cloned.1.call-start = ((), (), s32[]{:S(2)}) async-start(), calls=%async_computation.6 | async-start | bytes 2097152 | tf_op jit(solution)/shard_map/psum | solution.py:44
  771.3 216.4 %all-reduce.19.cloned.1.call-start = ((), (), s32[]{:S(2)}) async-start(), calls=%async_computation.1 | async-start | bytes 1835008 | tf_op jit(solution)/shard_map/psum | solution.py:39
  870.5 215.2 %all-reduce.27.cloned.1.call-start = ((), (), s32[]{:S(2)}) async-start(), calls=%async_computation.5 | async-start | bytes 2097152 | tf_op jit(solution)/shard_map/psum | solution.py:44
Sparse Core Ops, SparseCore 0:
  10.4 165.4 all-gather.1
  204.4 116.8 all-reduce.24
  327.2 92.1 all-reduce.32
  426.4 117.0 all-reduce.22
  549.4 92.0 all-reduce.30
  648.5 117.0 all-reduce.20
  771.4 92.1 all-reduce.28
  870.6 117.0 all-reduce.18
  993.6 92.0 all-reduce.26
where the time goes:
time: 1090 us
  waiting for transfers between devices  1000 us (92%)
  matrix products  41.1 us (4%)
  local copies, waits for them, and re-layouts  27.3 us (3%)
  between operations  13.9 us (1%)
  other arithmetic  11.5 us (1%)
    psum x4, waiting for transfers between devices, template_update(): num_a, den_a = lax.psum((num_t, den_t), 'spec')  468 us
    psum x4, waiting for transfers between devices, coef_update(): num_a, den_a = lax.psum((num_c, den_c), 'wave')  368 us
    all_gather x1, waiting for transfers between devices, shards(): whole = lax.all_gather(spectra, 'wave', axis=1, tiled=True)  163 us
    dot_general x8, matrix products, over_rows(): lax.dot_general(left, right, (((0,), (0,)), ((), ())), preferred_element_...  23.1 us
  transfers between devices with their start and end apart: 9, of which 9 were waited for; matrix products, arithmetic and copies ran while one was open for 1% of the time, Pallas kernels for 0%

commit v1 on v0

v1 whole, which is shorter than its diff:
```python
import functools

import jax
import jax.numpy as jnp
from jax import lax
from jax.experimental import pallas as pl
from jax.experimental.pallas import tpu as pltpu
from jax.sharding import Mesh, PartitionSpec as P

ITERS = 4
PIX = 7168
RANK = 128
ROWS = 128
BOTH = 2 * ROWS
N_WAVE = 8
WIDTH = PIX // N_WAVE
CHIPS = 64
RUN = 56
MINE = CHIPS * RUN
STEP = 448
CODES = 32000.0
TINY = 1e-37

AXES = ("ylo", "x", "core", "zh", "zl", "yhi")
SPEC = ("ylo", "x", "core")
WAVE = ("zh", "zl", "yhi")
CHIP = ("zh", "zl", "yhi", "ylo", "x")

PARAMS = pltpu.CompilerParams(vmem_limit_bytes=56 * 1024 * 1024)
VM = pl.BlockSpec(memory_space=pltpu.VMEM)
SM = pl.BlockSpec(memory_space=pltpu.SMEM)


def shift_kernel(off_ref, obs_ref, lo_ref, hi_ref, out_ref, held):
    for w in range(N_WAVE):
        held[pl.ds(w * WIDTH, WIDTH), :] = obs_ref[w, pl.ds(0, WIDTH), :]
    held[pl.ds(PIX, 128), :] = jnp.zeros((128, ROWS), jnp.bfloat16)
    off = off_ref[0]
    fine = lax.rem(off, 16)
    coarse = off - fine
    lo = lo_ref[...]
    hi = hi_ref[...]
    row = lax.broadcasted_iota(jnp.int32, (2 * RUN, ROWS), 0)
    back = lax.rem(128 - fine, 128)

    def step(m, carry):
        first = 2 * RUN * m
        at = pl.multiple_of(jnp.minimum(first + coarse, PIX), 16)
        piece = held[pl.ds(at, 128), :].astype(jnp.float32)
        piece = pltpu.roll(piece, back, 0)[: 2 * RUN]
        seen = row + (first + off)
        inside = (seen >= lo) & (seen < hi)
        piece = jnp.where(inside, piece, 0.0)
        out_ref[0, m] = piece[:RUN].astype(jnp.bfloat16)
        out_ref[1, m] = piece[RUN:].astype(jnp.bfloat16)
        return carry

    lax.fori_loop(0, CHIPS, step, 0)


def ratio_of(own_ref, oth_ref, wt, hb, rows):
    model = jnp.dot(wt, hb, preferred_element_type=jnp.float32)
    rest = jnp.concatenate([own_ref[rows, :], oth_ref[rows, :]], axis=1).astype(jnp.float32)
    model = jnp.maximum(model, TINY)
    inv = pl.reciprocal(model, approx=True)
    inv = inv * (2.0 - model * inv)
    ratio = (rest * inv).astype(jnp.bfloat16)
    weight = jnp.where(rest > 0, 1.0, 0.0).astype(jnp.bfloat16)
    return ratio, weight


def swapped(x):
    return jnp.concatenate([x[:, ROWS:], x[:, :ROWS]], axis=1)


def template_kernel(first, *refs):
    if first:
        own_ref, oth_ref, wt_ref, ht_ref, out_ref, num_s, den_s = refs
        ht = ht_ref[...]
    else:
        own_ref, oth_ref, wt_ref, ht_ref, nd_ref, nd_oth_ref, out_ref, ht_out_ref, num_s, den_s = refs
        num = nd_ref[0] + swapped(nd_oth_ref[0])
        den = nd_ref[1] + swapped(nd_oth_ref[1])
        ht = ht_ref[...] * num / jnp.maximum(den, 1.0)
        ht_out_ref[...] = ht
    hb = ht.astype(jnp.bfloat16)

    def chunk(k, carry):
        top_n, top_d = carry
        rows = pl.ds(pl.multiple_of(k * STEP, STEP), STEP)
        ratio, weight = ratio_of(own_ref, oth_ref, wt_ref[rows, :], hb, rows)
        dims = (((1,), (1,)), ((), ()))
        num = lax.dot_general(ratio, hb, dims, preferred_element_type=jnp.float32)
        den = lax.dot_general(weight, hb, dims, preferred_element_type=jnp.float32)
        num_s[rows, :] = num
        den_s[rows, :] = den
        top_n = jnp.maximum(top_n, jnp.max(num.reshape(STEP // 8, 8, RANK), axis=0))
        top_d = jnp.maximum(top_d, jnp.max(den.reshape(STEP // 8, 8, RANK), axis=0))
        return top_n, top_d

    zero = jnp.zeros((8, RANK), jnp.float32)
    top_n, top_d = lax.fori_loop(0, MINE // STEP, chunk, (zero, zero))

    def power(top):
        top = jnp.max(top, axis=0, keepdims=True)
        power = jnp.ceil(jnp.log(jnp.maximum(top, 1e-30)) * 1.4426950408889634)
        return jnp.broadcast_to(power, (8, RANK))

    pow_n, pow_d = power(top_n), power(top_d)
    tail = jnp.concatenate([pow_n, pow_d], axis=0).astype(jnp.int32).astype(jnp.int16)
    scale_n = jnp.exp2(-pow_n) * CODES
    scale_d = jnp.exp2(-pow_d) * CODES

    def code(m, carry):
        rows = pl.ds(pl.multiple_of(m * RUN, 8), RUN)
        num = num_s[rows, :].reshape(RUN // 8, 8, RANK) * scale_n[None] + 0.5
        den = den_s[rows, :].reshape(RUN // 8, 8, RANK) * scale_d[None] + 0.5
        both = jnp.concatenate([num.reshape(RUN, RANK), den.reshape(RUN, RANK)], axis=0)
        out_ref[m, pl.ds(0, 2 * RUN), :] = both.astype(jnp.int32).astype(jnp.int16)
        out_ref[m, pl.ds(2 * RUN, 16), :] = tail
        return carry

    lax.fori_loop(0, CHIPS, code, 0, unroll=4)


def update_kernel(got_ref, w_ref, w_out_ref, send_ref):
    def add(j, carry):
        num, den = carry
        power = got_ref[j, pl.ds(2 * RUN, 16), :].astype(jnp.int32).astype(jnp.float32)
        scale = jnp.exp2(power) * (1.0 / CODES)
        both = got_ref[j, pl.ds(0, 2 * RUN), :].astype(jnp.int32).astype(jnp.float32)
        num = num + both[:RUN].reshape(RUN // 8, 8, RANK) * scale[None, :8]
        den = den + both[RUN:].reshape(RUN // 8, 8, RANK) * scale[None, 8:]
        return num, den

    zero = jnp.zeros((RUN // 8, 8, RANK), jnp.float32)
    num, den = lax.fori_loop(0, CHIPS, add, (zero, zero), unroll=4)
    num = num.reshape(RUN, RANK)
    den = den.reshape(RUN, RANK)
    w = w_ref[...] * num / jnp.maximum(den, 1.0)
    w_out_ref[...] = w
    sent = w.astype(send_ref.dtype)
    for j in range(CHIPS):
        send_ref[j] = sent


def coef_kernel(own_ref, oth_ref, wt_ref, ht_ref, nd_ref):
    hb = ht_ref[...].astype(jnp.bfloat16)

    def chunk(k, carry):
        num, den = carry
        rows = pl.ds(pl.multiple_of(k * STEP, STEP), STEP)
        wt = wt_ref[rows, :].astype(jnp.bfloat16)
        ratio, weight = ratio_of(own_ref, oth_ref, wt, hb, rows)
        dims = (((0,), (0,)), ((), ()))
        num = num + lax.dot_general(wt, ratio, dims, preferred_element_type=jnp.float32)
        den = den + lax.dot_general(wt, weight, dims, preferred_element_type=jnp.float32)
        return num, den

    zero = jnp.zeros((RANK, BOTH), jnp.float32)
    num, den = lax.fori_loop(0, MINE // STEP, chunk, (zero, zero))
    nd_ref[0] = num
    nd_ref[1] = den


def call(kernel, n_in, outs, scratch=(), smem=0):
    shapes = [jax.ShapeDtypeStruct(s, d) for s, d in outs]
    return pl.pallas_call(
        kernel,
        out_shape=shapes,
        in_specs=[SM] * smem + [VM] * (n_in - smem),
        out_specs=[VM] * len(shapes),
        scratch_shapes=list(scratch),
        compiler_params=PARAMS,
    )


def to_partner(x):
    return lax.ppermute(x, "core", [(0, 1), (1, 0)])


def shards(spectra, offsets, cover_lo, cover_hi, coefficients, templates):
    bf = jnp.bfloat16
    f32 = jnp.float32
    core = lax.axis_index("core")
    wave = lax.axis_index(WAVE)
    spec = lax.axis_index(SPEC)

    temps_t = templates.T
    runs = temps_t.reshape(N_WAVE, 2, RUN, RANK)
    first_w = lax.dynamic_index_in_dim(runs, core, 1, keepdims=False).reshape(WIDTH // 2, RANK)
    flux_t = spectra.reshape(N_WAVE, ROWS, WIDTH).transpose(0, 2, 1)
    first_b = jnp.broadcast_to(first_w.astype(bf)[None], (N_WAVE, WIDTH // 2, RANK))
    got = lax.all_to_all(jnp.concatenate([flux_t, first_b], axis=1), WAVE, 0, 0, tiled=True)
    wt = got[:, WIDTH:].reshape(MINE, RANK)
    w_own = lax.dynamic_slice_in_dim(temps_t, spec * RUN, RUN, 0)

    start = wave * ROWS
    off = lax.dynamic_slice_in_dim(offsets, wave // 2, 1, 0)
    lo = lax.dynamic_slice_in_dim(cover_lo, start, ROWS, 0).reshape(1, ROWS)
    hi = lax.dynamic_slice_in_dim(cover_hi, start, ROWS, 0).reshape(1, ROWS)
    (rest,) = call(
        shift_kernel,
        4,
        [((2, CHIPS, RUN, ROWS), bf)],
        [pltpu.VMEM((PIX + 128, ROWS), bf)],
        smem=1,
    )(off, got, lo, hi)
    rest = rest.reshape(2, MINE, ROWS)
    own = lax.dynamic_index_in_dim(rest, core, 0, keepdims=False)
    oth = to_partner(lax.dynamic_index_in_dim(rest, 1 - core, 0, keepdims=False))

    h_own = lax.dynamic_slice_in_dim(coefficients, start, ROWS, 0).T
    ht = jnp.concatenate([h_own, to_partner(h_own)], axis=1)

    codes = ((CHIPS, 2 * RUN + 16, RANK), jnp.int16)
    nd_shape = ((2, RANK, BOTH), f32)
    stats = [pltpu.VMEM((MINE, RANK), f32)] * 2
    for update in range(ITERS):
        if update == 0:
            (sums,) = call(functools.partial(template_kernel, True), 4, [codes], stats)(own, oth, wt, ht)
        else:
            sums, ht = call(
                functools.partial(template_kernel, False), 6, [codes, ((RANK, BOTH), f32)], stats
            )(own, oth, wt, ht, nd, nd_oth)
        got_sums = lax.all_to_all(sums, CHIP, 0, 0, tiled=True)
        sent = f32 if update == ITERS - 1 else bf
        w_own, send = call(
            update_kernel, 2, [((RUN, RANK), f32), ((CHIPS, RUN, RANK), sent)]
        )(got_sums, w_own)
        wt = lax.all_to_all(send, CHIP, 0, 0, tiled=True).reshape(MINE, RANK)
        (nd,) = call(coef_kernel, 4, [nd_shape])(own, oth, wt, ht)
        if update < ITERS - 1:
            nd_oth = to_partner(nd)

    mine = lax.dynamic_slice_in_dim(wt, wave * (WIDTH // 2), WIDTH // 2, 0)
    theirs = to_partner(mine)
    even = jnp.where(core == 0, mine, theirs).reshape(N_WAVE, 1, RUN, RANK)
    odd = jnp.where(core == 0, theirs, mine).reshape(N_WAVE, 1, RUN, RANK)
    temps = jnp.concatenate([even, odd], axis=1).reshape(WIDTH, RANK).T

    nd_half = nd[:, :, :ROWS] + to_partner(nd[:, :, ROWS:])
    h_new = (ht[:, :ROWS] * nd_half[0] / jnp.maximum(nd_half[1], 1.0)).T
    coef = lax.all_to_all(
        jnp.broadcast_to(h_new[None], (N_WAVE, ROWS, RANK)), WAVE, 0, 0, tiled=True
    ).reshape(N_WAVE * ROWS, RANK)
    return (temps, coef)


def solution(mesh):
    fine = Mesh(mesh.devices.reshape(2, 4, 2, 2, 2, 2), AXES)
    in_specs = (
        P(SPEC, WAVE),
        P(SPEC),
        P(SPEC),
        P(SPEC),
        P(SPEC, None),
        P(None, WAVE),
    )
    out_specs = (P(None, WAVE), P(SPEC, None))
    return jax.shard_map(shards, mesh=fine, in_specs=in_specs, out_specs=out_specs, check_vma=False)
```

time: 1090 us -> 415 us (0.38)
  waiting for transfers between devices: 1000 us -> 79.6 us
  blocking collectives: 0 us -> 211 us
  Pallas kernels: 0 us -> 75.3 us
  matrix products: 41.1 us -> 0 us
  starting transfers between devices: 0.77 us -> 19.2 us
  between operations: 13.9 us -> 0.82 us
    psum x8 -> x0, waiting for transfers between devices: 836 us -> none  [the longest x4 468 us: template_update(): num_a, den_a = lax.psum((num_t, den_t), 'spec')]
    all_to_all x0 -> x7, blocking collectives: none -> 211 us  [the longest x3 108 us: shards(): got_sums = lax.all_to_all(sums, CHIP, 0, 0, tiled=True)]
    all_gather x1 -> x0, waiting for transfers between devices: 163 us -> none  [shards(): whole = lax.all_gather(spectra, 'wave', axis=1, tiled=True)]
    pallas_call x0 -> x13, Pallas kernels: none -> 75.3 us  [the longest x4 26.5 us: shards(): nd, = call(coef_kernel, 4, [nd_shape])(own, oth, wt, ht)]
    all_to_all x0 -> x3, waiting for transfers between devices: none -> 72.5 us  [the longest x1 33.6 us: shards(): lax.all_to_all(jnp.concatenate([flux_t, first_b], axis=1), WAVE, 0, 0, ti...]
    dot_general x16 -> x0, matrix products: 41.1 us -> none  [the longest x8 23.1 us: over_rows(): lax.dot_general(left, right, (((0,), (0,)), ((), ())), preferred_element_...]
    all_to_all x0 -> x3, starting transfers between devices: none -> 18 us  [the longest x1 8.16 us: shards(): lax.all_to_all(jnp.concatenate([flux_t, first_b], axis=1), WAVE, 0, 0, ti...]
    concatenate x1 -> x0, local copies, waits for them, and re-layouts: 12.9 us -> none  [shards(): jnp.concatenate([whole, jnp.zeros((rows, width), whole.dtype)], axis=1)]
  transfers between devices with their start and end apart: 9 -> 10, of which waited for: 9 -> 7; matrix products, arithmetic and copies ran while one was open for 1% -> 3% of each run, Pallas kernels for 0% -> 0%
where the time goes in v1:
time: 415 us; the launch traced here: 413 us
  blocking collectives  211 us (51%)
  waiting for transfers between devices  79.6 us (19%)
  Pallas kernels  75.3 us (18%)
  local copies, waits for them, and re-layouts  23.4 us (6%)
  starting transfers between devices  19.2 us (5%)
  other arithmetic  4.32 us (1%)
    all_to_all x3, blocking collectives, shards(): got_sums = lax.all_to_all(sums, CHIP, 0, 0, tiled=True)  108 us
    all_to_all x4, blocking collectives, shards(): wt = lax.all_to_all(send, CHIP, 0, 0, tiled=True).reshape(MINE, RANK)  102 us
    all_to_all x1, waiting for transfers between devices, shards(): lax.all_to_all(jnp.concatenate([flux_t, first_b], axis=1), WAVE, 0, 0, ti...  33.6 us
    all_to_all x1, waiting for transfers between devices, shards(): got_sums = lax.all_to_all(sums, CHIP, 0, 0, tiled=True)  29 us
    pallas_call x4, Pallas kernels, shards(): nd, = call(coef_kernel, 4, [nd_shape])(own, oth, wt, ht)  26.5 us
    pallas_call x3, Pallas kernels, shards(): call(functools.partial(template_kernel, False), 6, [codes, ((RANK, BOTH),...  22.5 us
    pallas_call x4, Pallas kernels, shards(): call(update_kernel, 2, [((RUN, RANK), f32), ((CHIPS, RUN, RANK), sent)])  13.3 us
    all_to_all x1, waiting for transfers between devices, shards(): lax.all_to_all(jnp.broadcast_to(h_new[None], (N_WAVE, ROWS, RANK)), WAVE,...  9.98 us
  transfers between devices with their start and end apart: 10, of which 7 were waited for; matrix products, arithmetic and copies ran while one was open for 3% of the time, Pallas kernels for 0%

profile of v1, /device:TPU:0, one launch (start us, length us, event | category | flops | bytes accessed | tf_op | source)
XLA Modules:
  0.0 413.2 jit_solution(16599099158136746655)
XLA Ops:
  0.6 0.0 copy-start
  0.7 1.3 copy.14
  1.9 0.0 copy-start.4
  1.9 3.3 copy.13
  5.3 0.1 broadcast_in_dim.4
  5.4 1.7 pad_maximum_fusion
  7.2 8.2 %all-to-all-start = ((bf16[8,1344,128]{2,1,0:T(8,128)(2,1)}), bf16[8,1344,128]{2,1,0:T(8,128)(2,1)S(1)}, u32[]{:S(2)}, u32[]{:S(2)}) async-start(bf16[8,1344,128]{2,1,0:T(8,128)(2,1)} %pad_maximum_fusion), calls=%async_computation | async-start | bytes 5505024 | tf_op jit(solution)/shard_map/all_to_all | solution.py:194
  15.3 0.6 dynamic_slice.29.off_ref
  15.9 1.4 dynamic-slice_bitcast_fusion.3
  17.3 33.6 %all-to-all-done.obs_ref = bf16[8,1344,128]{2,1,0:T(8,128)(2,1)S(1)} async-done(((bf16[8,1344,128]{2,1,0:T(8,128)(2,1)}), bf16[8,1344,128]{2,1,0:T(8,128)(2,1)S(1)}, u32[]{:S(2)}, u32[]{:S(2)}) %all-to-all-start) | async-done | bytes 2752544 | tf_op jit(solution)/shard_map/all_to_all | solution.py:194
  50.8 1.5 copy-done.2
  52.3 5.8 %shard_map.77 = bf16[2,64,56,128]{3,2,1,0:T(8,128)(2,1)} custom-call(s32[1]{0:T(128)} %dynamic_slice.29.off_ref, bf16[8,1344,128]{2,1,0:T(8,128)(2,1)} %copy-done.2, s32[1,128]{1,0:T(1,128)} %get-tuple-element.35.lo_ref, s32[1,128]{1,0:T(1,128)} %get-tuple-element.34.hi_ref), custom_call_target="tpu_custom_call" | custom-call | tf_op jit(solution)/shard_map/pallas_call | solution.py:202
  58.1 2.5 dynamic-slice_bitcast_fusion
  60.7 0.0 collective-permute-start
  60.7 0.1 copy.21
  60.8 0.6 collective-permute-start.1
  61.4 1.9 collective-permute-done.1
  63.2 0.7 pad_maximum_fusion.2.refs_3_.ht_ref
  63.9 2.2 slice.24
  66.1 0.0 collective-permute-done.refs_1_.oth_ref
  66.1 0.9 copy-done.1
  67.0 7.3 %shard_map.78 = s16[64,128,128]{2,1,0:T(8,128)(2,1)} custom-call(bf16[3584,128]{1,0:T(8,128)(2,1)} %get-tuple-element.31.refs_0_.own_ref, bf16[3584,128]{1,0:T(8,128)(2,1)} %copy-done.1, bf16[3584,128]{1,0:T(8,128)(2,1)} %bitcast.58, f32[128,256]{1,0:T(8,128)} %pad_maximum_fusion.2.refs_3_.ht_ref), custom_call_target="tpu_custom_call" | custom-call | tf_op jit(solution)/shard_map/pallas_call | solution.py:221
  74.3 6.3 %all-to-all-start.1 = ((s16[64,128,128]{2,1,0:T(8,128)(2,1)}), s16[64,128,128]{2,1,0:T(8,128)(2,1)S(1)}, u32[]{:S(2)}, u32[]{:S(2)}) async-start(s16[64,128,128]{2,1,0:T(8,128)(2,1)} %shard_map.78), calls=%async_computation.1 | async-start | bytes 4194304 | tf_op jit(solution)/shard_map/all_to_all | solution.py:226
  80.7 1.4 dynamic-slice_bitcast_fusion.2.w_ref
  82.0 29.0 %all-to-all-done.1.got_ref = s16[64,128,128]{2,1,0:T(8,128)(2,1)S(1)} async-done(((s16[64,128,128]{2,1,0:T(8,128)(2,1)}), s16[64,128,128]{2,1,0:T(8,128)(2,1)S(1)}, u32[]{:S(2)}, u32[]{:S(2)}) %all-to-all-start.1) | async-done | bytes 2097184 | tf_op jit(solution)/shard_map/all_to_all | solution.py:226
  111.0 1.4 copy-done.3
  112.4 3.2 shard_map.79
  115.6 23.2 %all_to_all.50 = bf16[64,56,128]{2,1,0:T(8,128)(2,1)} all-to-all(bf16[64,56,128]{2,1,0:T(8,128)(2,1)} %get-tuple-element.15), channel_id=1, replica_groups=mesh['ylo'=2,'x'=4,'core'=2,'zh'=2,'zl'=2,'yhi'=2] {'zh','zl','yhi','ylo..., dimensions={0} | all-to-all | bytes 1835008 | tf_op jit(solution)/shard_map/all_to_all | solution.py:231
  138.8 6.5 %shard_map.80.refs_4_ = f32[2,128,256]{2,1,0:T(8,128)} custom-call(bf16[3584,128]{1,0:T(8,128)(2,1)} %get-tuple-element.31.refs_0_.own_ref, bf16[3584,128]{1,0:T(8,128)(2,1)} %copy-done.1, bf16[3584,128]{1,0:T(8,128)(2,1)} %bitcast.54, f32[128,256]{1,0:T(8,128)} %pad_maximum_fusion.2.refs_3_.ht_ref), custom_call_target="tpu_custom_call" | custom-call | tf_op jit(solution)/shard_map/pallas_call | solution.py:232
  145.3 1.7 collective-permute-done.2.refs_5_
  147.1 0.7 copy-done.6
  147.8 7.5 %shard_map.81 = (s16[64,128,128]{2,1,0:T(8,128)(2,1)}, f32[128,256]{1,0:T(8,128)}) custom-call(bf16[3584,128]{1,0:T(8,128)(2,1)} %get-tuple-element.31.refs_0_.own_ref, bf16[3584,128]{1,0:T(8,128)(2,1)} %copy-done.1, bf16[3584,128]{1,0:T(8,128)(2,1)} %bitcast.55, f32[128,256]{1,0:T(8,128)} %pad_maximum_fusion.2.refs_3_.ht_ref, ...), custom_call_target="tpu_custom_call" | custom-call | tf_op jit(solution)/shard_map/pallas_call | solution.py:223
  155.3 36.2 %all_to_all.51.got_ref = s16[64,128,128]{2,1,0:T(8,128)(2,1)} all-to-all(s16[64,128,128]{2,1,0:T(8,128)(2,1)} %get-tuple-element.16), channel_id=1, replica_groups=mesh['ylo'=2,'x'=4,'core'=2,'zh'=2,'zl'=2,'yhi'=2] {'zh','zl','yhi','ylo..., dimensions={0} | all-to-all | bytes 4194304 | tf_op jit(solution)/shard_map/all_to_all | solution.py:226
  191.4 3.2 shard_map.82
  194.7 23.0 %all_to_all.52 = bf16[64,56,128]{2,1,0:T(8,128)(2,1)} all-to-all(bf16[64,56,128]{2,1,0:T(8,128)(2,1)} %get-tuple-element.18), channel_id=1, replica_groups=mesh['ylo'=2,'x'=4,'core'=2,'zh'=2,'zl'=2,'yhi'=2] {'zh','zl','yhi','ylo..., dimensions={0} | all-to-all | bytes 1835008 | tf_op jit(solution)/shard_map/all_to_all | solution.py:231
  217.7 6.5 %shard_map.83.refs_4_ = f32[2,128,256]{2,1,0:T(8,128)} custom-call(bf16[3584,128]{1,0:T(8,128)(2,1)} %get-tuple-element.31.refs_0_.own_ref, bf16[3584,128]{1,0:T(8,128)(2,1)} %copy-done.1, bf16[3584,128]{1,0:T(8,128)(2,1)} %bitcast.50, f32[128,256]{1,0:T(8,128)} %get-tuple-element.19.ht_ref.refs_3_), custom_call_target="tpu_custom_call" | custom-call | tf_op jit(solution)/shard_map/pallas_call | solution.py:232
  224.3 0.0 collective-permute-start.3
  224.3 1.7 collective-permute-done.3.refs_5_
  226.0 0.7 copy-done.7
  226.7 7.5 %shard_map.84 = (s16[64,128,128]{2,1,0:T(8,128)(2,1)}, f32[128,256]{1,0:T(8,128)}) custom-call(bf16[3584,128]{1,0:T(8,128)(2,1)} %get-tuple-element.31.refs_0_.own_ref, bf16[3584,128]{1,0:T(8,128)(2,1)} %copy-done.1, bf16[3584,128]{1,0:T(8,128)(2,1)} %bitcast.51, f32[128,256]{1,0:T(8,128)} %get-tuple-element.19.ht_ref.refs_3_, ...), custom_call_target="tpu_custom_call" | custom-call | tf_op jit(solution)/shard_map/pallas_call | solution.py:223
  234.2 36.2 %all_to_all.53.got_ref = s16[64,128,128]{2,1,0:T(8,128)(2,1)} all-to-all(s16[64,128,128]{2,1,0:T(8,128)(2,1)} %get-tuple-element.20), channel_id=1, replica_groups=mesh['ylo'=2,'x'=4,'core'=2,'zh'=2,'zl'=2,'yhi'=2] {'zh','zl','yhi','ylo..., dimensions={0} | all-to-all | bytes 4194304 | tf_op jit(solution)/shard_map/all_to_all | solution.py:226
  270.3 3.2 shard_map.85
  273.6 23.0 %all_to_all.54 = bf16[64,56,128]{2,1,0:T(8,128)(2,1)} all-to-all(bf16[64,56,128]{2,1,0:T(8,128)(2,1)} %get-tuple-element.22), channel_id=1, replica_groups=mesh['ylo'=2,'x'=4,'core'=2,'zh'=2,'zl'=2,'yhi'=2] {'zh','zl','yhi','ylo..., dimensions={0} | all-to-all | bytes 1835008 | tf_op jit(solution)/shard_map/all_to_all | solution.py:231
  296.6 6.5 %shard_map.86.refs_4_ = f32[2,128,256]{2,1,0:T(8,128)} custom-call(bf16[3584,128]{1,0:T(8,128)(2,1)} %get-tuple-element.31.refs_0_.own_ref, bf16[3584,128]{1,0:T(8,128)(2,1)} %copy-done.1, bf16[3584,128]{1,0:T(8,128)(2,1)} %bitcast.52, f32[128,256]{1,0:T(8,128)} %get-tuple-element.23.ht_ref.refs_3_), custom_call_target="tpu_custom_call" | custom-call | tf_op jit(solution)/shard_map/pallas_call | solution.py:232
  303.2 0.0 collective-permute-start.4
  303.2 1.7 collective-permute-done.4.refs_5_
  304.9 0.7 copy-done.8
  305.6 7.5 %shard_map.87 = (s16[64,128,128]{2,1,0:T(8,128)(2,1)}, f32[128,256]{1,0:T(8,128)}) custom-call(bf16[3584,128]{1,0:T(8,128)(2,1)} %get-tuple-element.31.refs_0_.own_ref, bf16[3584,128]{1,0:T(8,128)(2,1)} %copy-done.1, bf16[3584,128]{1,0:T(8,128)(2,1)} %bitcast.53, f32[128,256]{1,0:T(8,128)} %get-tuple-element.23.ht_ref.refs_3_, ...), custom_call_target="tpu_custom_call" | custom-call | tf_op jit(solution)/shard_map/pallas_call | solution.py:223
  313.1 36.2 %all_to_all.55.got_ref = s16[64,128,128]{2,1,0:T(8,128)(2,1)} all-to-all(s16[64,128,128]{2,1,0:T(8,128)(2,1)} %get-tuple-element.24), channel_id=1, replica_groups=mesh['ylo'=2,'x'=4,'core'=2,'zh'=2,'zl'=2,'yhi'=2] {'zh','zl','yhi','ylo..., dimensions={0} | all-to-all | bytes 4194304 | tf_op jit(solution)/shard_map/all_to_all | solution.py:226
  349.3 3.6 shard_map.88
  352.9 32.7 %all_to_all.56 = f32[64,56,128]{2,1,0:T(8,128)} all-to-all(f32[64,56,128]{2,1,0:T(8,128)} %get-tuple-element.26), channel_id=1, replica_groups=mesh['ylo'=2,'x'=4,'core'=2,'zh'=2,'zl'=2,'yhi'=2] {'zh','zl','yhi','ylo..., dimensions={0} | all-to-all | bytes 3670016 | tf_op jit(solution)/shard_map/all_to_all | solution.py:231
  385.6 6.9 %shard_map.89 = f32[2,128,256]{2,1,0:T(8,128)} custom-call(bf16[3584,128]{1,0:T(8,128)(2,1)} %get-tuple-element.31.refs_0_.own_ref, bf16[3584,128]{1,0:T(8,128)(2,1)} %copy-done.1, f32[3584,128]{1,0:T(8,128)} %bitcast.47, f32[128,256]{1,0:T(8,128)} %get-tuple-element.27.ht_ref), custom_call_target="tpu_custom_call" | custom-call | tf_op jit(solution)/shard_map/pallas_call | solution.py:232
  392.5 0.9 slice.26
  393.4 0.1 collective-permute-start.6
  393.5 1.0 constant_dynamic-slice_fusion
  394.4 0.6 collective-permute-start.5
  395.0 0.9 slice_add_fusion
  396.0 0.1 copy.19
  396.1 0.8 broadcast_in_dim.5
  396.9 3.5 all-to-all-start.9
  400.4 1.0 broadcast_select_fusion.1
  401.5 1.0 copy.20
  402.4 10.0 %all-to-all-done.9 = f32[8,128,128]{2,1,0:T(8,128)S(1)} async-done(((f32[8,128,128]{2,1,0:T(8,128)}), f32[8,128,128]{2,1,0:T(8,128)S(1)}, u32[]{:S(2)}, u32[]{:S(2)}) %all-to-all-start.9) | async-done | bytes 524320 | tf_op jit(solution)/shard_map/all_to_all | solution.py:244
  412.4 0.8 copy.23
  (19 shorter events, 0.1 us)
Async XLA Ops:
  0.6 60.0 %copy-start = (f32[1024,128]{1,0:T(8,128)S(1)}, f32[1024,128]{1,0:T(8,128)}, u32[]{:S(2)}) copy-start(f32[1024,128]{1,0:T(8,128)} %param.10) | copy-start | bytes 1572868
  1.9 3.5 copy-start.4
  7.2 8.2 %copy-start.9 = (s32[4]{0:T(128)S(1)}, s32[4]{0:T(128)}, u32[]{:S(2)}) copy-start(s32[4]{0:T(128)} %param.7) | copy-start | bytes 52
  7.2 43.7 %all-to-all-start = ((bf16[8,1344,128]{2,1,0:T(8,128)(2,1)}), bf16[8,1344,128]{2,1,0:T(8,128)(2,1)S(1)}, u32[]{:S(2)}, u32[]{:S(2)}) async-start(bf16[8,1344,128]{2,1,0:T(8,128)(2,1)} %pad_maximum_fusion), calls=%async_computation | async-start | bytes 5505024 | tf_op jit(solution)/shard_map/all_to_all | solution.py:194
  50.8 1.5 copy-start.2
  60.7 5.4 %collective-permute-start = (bf16[3584,128]{1,0:T(8,128)(2,1)S(1)}, bf16[3584,128]{1,0:T(8,128)(2,1)S(1)}, u32[]{:S(2)}, u32[]{:S(2)}) collective-permute-start(bf16[3584,128]{1,0:T(8,128)(2,1)S(1)} %get-tuple-element.30), channel_id=1, source_target_pairs={{0,8},{8,0},{1,9},{9,1},{2,10},{10,2},{3,11},{11,3},{4,12},{12,4},... | collective-permute-start | bytes 2752520 | tf_op jit(solution)/shard_map/ppermute | solution.py:179
  60.8 2.5 collective-permute-start.1
  66.1 0.9 copy-start.1
  74.3 36.7 %all-to-all-start.1 = ((s16[64,128,128]{2,1,0:T(8,128)(2,1)}), s16[64,128,128]{2,1,0:T(8,128)(2,1)S(1)}, u32[]{:S(2)}, u32[]{:S(2)}) async-start(s16[64,128,128]{2,1,0:T(8,128)(2,1)} %shard_map.78), calls=%async_computation.1 | async-start | bytes 4194304 | tf_op jit(solution)/shard_map/all_to_all | solution.py:226
  111.0 1.4 copy-start.3
  145.3 1.7 collective-permute-start.2
  147.1 0.7 copy-start.6
  224.3 1.7 collective-permute-start.3
  226.0 0.7 copy-start.7
  303.2 1.7 collective-permute-start.4
  304.9 0.7 copy-start.8
  385.6 10.4 %copy-start.5 = (f32[128,256]{1,0:T(8,128)S(1)}, f32[128,256]{1,0:T(8,128)}, u32[]{:S(2)}) copy-start(f32[128,256]{1,0:T(8,128)} %get-tuple-element.27.ht_ref) | copy-start | bytes 393220
  393.4 1.6 collective-permute-start.6
  394.4 6.0 %collective-permute-start.5 = (f32[448,128]{1,0:T(8,128)S(1)}, f32[448,128]{1,0:T(8,128)S(1)}, u32[]{:S(2)}, u32[]{:S(2)}) collective-permute-start(f32[448,128]{1,0:T(8,128)S(1)} %constant_dynamic-slice_fusion), channel_id=1, source_target_pairs={{0,8},{8,0},{1,9},{9,1},{2,10},{10,2},{3,11},{11,3},{4,12},{12,4},... | collective-permute-start | bytes 688136 | tf_op jit(solution)/shard_map/ppermute | solution.py:179
  396.9 15.5 %all-to-all-start.9 = ((f32[8,128,128]{2,1,0:T(8,128)}), f32[8,128,128]{2,1,0:T(8,128)S(1)}, u32[]{:S(2)}, u32[]{:S(2)}) async-start(f32[8,128,128]{2,1,0:T(8,128)} %broadcast_in_dim.5), calls=%async_computation.9 | async-start | bytes 1048576 | tf_op jit(solution)/shard_map/all_to_all | solution.py:244

commit v2 on v1

v2 whole, which is shorter than its diff:
```python
import functools

import jax
import jax.numpy as jnp
from jax import lax
from jax.experimental import pallas as pl
from jax.experimental.pallas import tpu as pltpu
from jax.sharding import Mesh, PartitionSpec as P

ITERS = 4
PIX = 7168
RANK = 128
ROWS = 128
PAIR = 2 * ROWS
HELD = 4 * ROWS
N_WAVE = 8
WIDTH = PIX // N_WAVE
CHIPS = 32
RUN = 56
MINE = CHIPS * RUN
STEP = 448
TINY = 1e-37
LEVELS = 64000.0
MIDDLE = 32000.0
TAIL = 8
LOG2E = 1.4426950408889634

AXES = ("ylo", "x", "core", "zh", "zl", "yhi")
SPEC = ("ylo", "x", "core")
WAVE = ("zh", "zl", "yhi")
CHIP = ("zh", "zl", "ylo", "x")
FIRST = (((0,), (0,)), ((), ()))
LAST = (((1,), (1,)), ((), ()))

PARAMS = pltpu.CompilerParams(vmem_limit_bytes=16 * 1024 * 1024)
VM = pl.BlockSpec(memory_space=pltpu.VMEM)
SM = pl.BlockSpec(memory_space=pltpu.SMEM)


def to_int(x):
    return x.astype(jnp.int32)


def scale_of(top):
    return jnp.ceil(jnp.log(jnp.maximum(top, 1e-30)) * (64 * LOG2E))


def codes_of(x, power):
    return to_int(x * (jnp.exp2(power * (-1 / 64)) * LEVELS) + 0.5) - int(MIDDLE)


def unit_of(power):
    return jnp.exp2(power * (1 / 64)) * (1 / LEVELS)


def tail_of(pow_a, pow_b):
    cols = pow_a.shape[1]
    half = (TAIL // 2, cols)
    return to_int(
        jnp.concatenate([jnp.broadcast_to(pow_a, half), jnp.broadcast_to(pow_b, half)], axis=0)
    )


def coded(num, den):
    pow_n = scale_of(jnp.max(num, axis=0, keepdims=True))
    pow_d = scale_of(jnp.max(den, axis=0, keepdims=True))
    return jnp.concatenate(
        [codes_of(num, pow_n), codes_of(den, pow_d), tail_of(pow_n, pow_d)], axis=0
    ).astype(jnp.int16)


def decoded(codes):
    x = codes.astype(jnp.int32).astype(jnp.float32)
    rows = (x.shape[0] - TAIL) // 2
    unit_n = unit_of(x[2 * rows : 2 * rows + 1])
    unit_d = unit_of(x[2 * rows + TAIL // 2 : 2 * rows + TAIL // 2 + 1])
    return (x[:rows] + MIDDLE) * unit_n, (x[rows : 2 * rows] + MIDDLE) * unit_d


def coded_one(x):
    power = scale_of(jnp.max(x, axis=0, keepdims=True))
    return jnp.concatenate([codes_of(x, power), tail_of(power, power)], axis=0).astype(jnp.int16)


def decoded_one(codes):
    x = codes.astype(jnp.int32).astype(jnp.float32)
    rows = x.shape[0] - TAIL
    return (x[:rows] + MIDDLE) * unit_of(x[rows : rows + 1])


def shift_kernel(leave, sc_ref, obs_ref, lo_ref, hi_ref, a_ref, b_ref, held):
    for w in range(N_WAVE):
        held[pl.ds(w * WIDTH, WIDTH), :] = obs_ref[w]
    held[pl.ds(PIX, 128), :] = jnp.zeros((128, ROWS), jnp.bfloat16)
    off, core, side = sc_ref[0], sc_ref[1], sc_ref[2]
    if leave:
        side = 1 - side
    lo = lo_ref[...]
    hi = hi_ref[...]
    row = lax.broadcasted_iota(jnp.int32, (RUN, ROWS), 0)

    def step(k, carry):
        for out_ref, set_core in ((a_ref, core), (b_ref, 1 - core)):
            at = 2 * RUN * (k + 8 * (k // 8) + 8 * side) + RUN * set_core + off
            fine = lax.rem(at, 16)
            start = pl.multiple_of(jnp.minimum(at - fine, PIX), 16)
            piece = held[pl.ds(start, 80), :].astype(jnp.float32)
            piece = pltpu.roll(piece, lax.rem(80 - fine, 80), 0)[:RUN]
            seen = row + at
            piece = jnp.where((seen >= lo) & (seen < hi), piece, 0.0)
            out_ref[k] = piece.astype(jnp.bfloat16)
        return carry

    lax.fori_loop(0, CHIPS, step, 0, unroll=2)


def ratio_of(rest_refs, wt, hb, rows):
    model = jnp.dot(wt, hb, preferred_element_type=jnp.float32)
    rest = jnp.concatenate([ref[rows, :] for ref in rest_refs], axis=1).astype(jnp.float32)
    inv = pl.reciprocal(jnp.maximum(model, TINY), approx=True)
    ratio = (rest * inv).astype(jnp.bfloat16)
    weight = jnp.where(rest > 0, 1.0, 0.0).astype(jnp.bfloat16)
    return ratio, weight


def swapped(x):
    return jnp.concatenate([x[:, ROWS:], x[:, :ROWS]], axis=1)


def template_kernel(r0, r1, r2, r3, wt_ref, hb_ref, hb_oth_ref, out_ref, num_s, den_s):
    hb = jnp.concatenate([hb_ref[...], hb_oth_ref[...]], axis=1)

    def chunk(k, carry):
        top_n, top_d = carry
        rows = pl.ds(pl.multiple_of(k * STEP, STEP), STEP)
        ratio, weight = ratio_of((r0, r1, r2, r3), wt_ref[rows, :], hb, rows)
        num = lax.dot_general(ratio, hb, LAST, preferred_element_type=jnp.float32)
        den = lax.dot_general(weight, hb, LAST, preferred_element_type=jnp.float32)
        num_s[rows, :] = num
        den_s[rows, :] = den
        top_n = jnp.maximum(top_n, jnp.max(num.reshape(STEP // 8, 8, RANK), axis=0))
        top_d = jnp.maximum(top_d, jnp.max(den.reshape(STEP // 8, 8, RANK), axis=0))
        return top_n, top_d

    zero = jnp.zeros((8, RANK), jnp.float32)
    top_n, top_d = lax.fori_loop(0, MINE // STEP, chunk, (zero, zero))
    pow_n = scale_of(jnp.max(top_n, axis=0, keepdims=True))
    pow_d = scale_of(jnp.max(top_d, axis=0, keepdims=True))
    tail = tail_of(pow_n, pow_d)

    def code(m, carry):
        rows = pl.ds(pl.multiple_of(m * RUN, 8), RUN)
        num = codes_of(num_s[rows, :], pow_n)
        den = codes_of(den_s[rows, :], pow_d)
        out_ref[m] = jnp.concatenate([num, den, tail], axis=0).astype(jnp.int16)
        return carry

    lax.fori_loop(0, CHIPS, code, 0, unroll=4)


def update_kernel(last, got_ref, w_ref, w_out_ref, send_ref):
    def add(j, carry):
        num, den = decoded(got_ref[j])
        return carry[0] + num, carry[1] + den

    zero = jnp.zeros((RUN, RANK), jnp.float32)
    num, den = lax.fori_loop(0, CHIPS, add, (zero, zero), unroll=4)
    w = w_ref[...] * num / jnp.maximum(den, 1.0)
    w_out_ref[...] = w
    sent = coded_one(w) if last else w.astype(jnp.bfloat16)
    for j in range(CHIPS):
        send_ref[j] = sent


def unpack_kernel(codes_ref, wt_ref):
    def step(j, carry):
        wt_ref[j] = decoded_one(codes_ref[j]).astype(jnp.bfloat16)
        return carry

    lax.fori_loop(0, CHIPS, step, 0, unroll=4)


def coef_kernel(r0, r1, r2, r3, wt_ref, hb_ref, hb_oth_ref, keep_ref, give_ref):
    hb = jnp.concatenate([hb_ref[...], hb_oth_ref[...]], axis=1)

    def chunk(k, carry):
        num, den = carry
        rows = pl.ds(pl.multiple_of(k * STEP, STEP), STEP)
        wt = wt_ref[rows, :]
        ratio, weight = ratio_of((r0, r1, r2, r3), wt, hb, rows)
        num = num + lax.dot_general(wt, ratio, FIRST, preferred_element_type=jnp.float32)
        den = den + lax.dot_general(wt, weight, FIRST, preferred_element_type=jnp.float32)
        return num, den

    zero = jnp.zeros((RANK, HELD), jnp.float32)
    num, den = lax.fori_loop(0, MINE // STEP, chunk, (zero, zero))
    keep_ref[0] = num[:, :PAIR]
    keep_ref[1] = den[:, :PAIR]
    give_ref[0] = num[:, PAIR:]
    give_ref[1] = den[:, PAIR:]


def fold_kernel(a_ref, b_ref, out_ref):
    out_ref[...] = coded(a_ref[0] + b_ref[0], a_ref[1] + b_ref[1])


def fold_last_kernel(a_ref, b_ref, keep_ref, out_ref):
    num = a_ref[0] + b_ref[0]
    den = a_ref[1] + b_ref[1]
    keep_ref[0] = num[:, :ROWS]
    keep_ref[1] = den[:, :ROWS]
    out_ref[...] = coded(num[:, ROWS:], den[:, ROWS:])


def step_kernel(mine_ref, oth_ref, h_ref, h_out_ref, hb_out_ref):
    num, den = decoded(mine_ref[...])
    num_o, den_o = decoded(oth_ref[...])
    ht = h_ref[...] * (num + swapped(num_o)) / jnp.maximum(den + swapped(den_o), 1.0)
    h_out_ref[...] = ht
    hb_out_ref[...] = ht.astype(jnp.bfloat16)


def step_last_kernel(mine_ref, oth_ref, h_ref, out_ref):
    num, den = decoded(oth_ref[...])
    ht = h_ref[:, pl.ds(0, ROWS)] * (mine_ref[0] + num) / jnp.maximum(mine_ref[1] + den, 1.0)
    sent = coded_one(ht)
    for j in range(N_WAVE):
        out_ref[j] = sent


def coef_out_kernel(got_ref, out_ref):
    for j in range(N_WAVE):
        out_ref[pl.ds(j * ROWS, ROWS), :] = decoded_one(got_ref[j]).T


def temps_out_kernel(core_ref, mine_ref, theirs_ref, out_ref):
    swap = core_ref[0] == 1
    pieces = []
    for j in range(N_WAVE):
        mine = decoded_one(mine_ref[j])
        theirs = decoded_one(theirs_ref[j])
        pieces += [jnp.where(swap, theirs, mine), jnp.where(swap, mine, theirs)]
    whole = jnp.concatenate(pieces, axis=0)
    for j in range(WIDTH // 128):
        out_ref[:, pl.ds(j * 128, 128)] = whole[j * 128 : (j + 1) * 128].T


def call(kernel, n_in, outs, scratch=(), smem=0):
    shapes = [jax.ShapeDtypeStruct(s, d) for s, d in outs]
    return pl.pallas_call(
        kernel,
        out_shape=shapes,
        in_specs=[SM] * smem + [VM] * (n_in - smem),
        out_specs=[VM] * len(shapes),
        scratch_shapes=list(scratch),
        compiler_params=PARAMS,
    )


def over(axis, x):
    return lax.ppermute(x, axis, [(0, 1), (1, 0)])


def shards(spectra, offsets, cover_lo, cover_hi, coefficients, templates):
    bf = jnp.bfloat16
    f32 = jnp.float32
    i16 = jnp.int16
    core = lax.axis_index("core")
    side = lax.axis_index("yhi")
    wave = lax.axis_index(WAVE)
    spec = lax.axis_index(SPEC)

    flux_t = spectra.reshape(N_WAVE, ROWS, WIDTH).transpose(0, 2, 1)
    got = lax.all_to_all(flux_t, WAVE, 0, 0, tiled=True)

    start = wave * ROWS
    off = lax.dynamic_slice_in_dim(offsets, wave // 2, 1, 0)
    scalars = jnp.concatenate([off, core[None], side[None]])
    lo = lax.dynamic_slice_in_dim(cover_lo, start, ROWS, 0).reshape(1, ROWS)
    hi = lax.dynamic_slice_in_dim(cover_hi, start, ROWS, 0).reshape(1, ROWS)
    run = ((CHIPS, RUN, ROWS), bf)
    held = [pltpu.VMEM((PIX + 128, ROWS), bf)]
    leave, leave_core = call(functools.partial(shift_kernel, True), 4, [run] * 2, held, smem=1)(
        scalars, got, lo, hi
    )
    r1 = over("yhi", leave)
    r3 = over("yhi", over("core", leave_core))
    r0, stay_core = call(functools.partial(shift_kernel, False), 4, [run] * 2, held, smem=1)(
        scalars, got, lo, hi
    )
    r2 = over("core", stay_core)
    rest = [r.reshape(MINE, ROWS) for r in (r0, r1, r2, r3)]

    temps_t = templates.T
    runs = temps_t.reshape(N_WAVE, 2, RUN, RANK)
    first_w = lax.dynamic_index_in_dim(runs, core, 1, keepdims=False).reshape(WIDTH // 2, RANK)
    first_b = jnp.broadcast_to(first_w.astype(bf)[None], (4, WIDTH // 2, RANK))
    first_b, _ = lax.optimization_barrier((first_b, r0))
    wt = lax.all_to_all(first_b, ("zh", "zl"), 0, 0, tiled=True).reshape(MINE, RANK)
    w_own = lax.dynamic_slice_in_dim(temps_t, spec * RUN, RUN, 0)

    h_own = lax.dynamic_slice_in_dim(coefficients, start, ROWS, 0)
    h_oth = lax.dynamic_slice_in_dim(coefficients, (wave ^ 1) * ROWS, ROWS, 0)
    ht = jnp.concatenate([h_own, h_oth], axis=0).T
    hb = ht.astype(bf)

    sums_shape = ((CHIPS, 2 * RUN + TAIL, RANK), i16)
    nd_shape = ((2, RANK, PAIR), f32)
    stats = [pltpu.VMEM((MINE, RANK), f32)] * 2
    for update in range(ITERS):
        last = update == ITERS - 1
        hb_oth = over("core", hb)
        (sums,) = call(template_kernel, 7, [sums_shape], stats)(*rest, wt, hb, hb_oth)
        got_sums = lax.all_to_all(sums, CHIP, 0, 0, tiled=True)
        send_shape = ((CHIPS, RUN + TAIL, RANK), i16) if last else ((CHIPS, RUN, RANK), bf)
        w_own, send = call(
            functools.partial(update_kernel, last), 2, [((RUN, RANK), f32), send_shape]
        )(got_sums, w_own)
        wt = lax.all_to_all(send, CHIP, 0, 0, tiled=True)
        if last:
            w_codes = wt
            (wt,) = call(unpack_kernel, 1, [((CHIPS, RUN, RANK), bf)])(wt)
        wt = wt.reshape(MINE, RANK)
        keep, give = call(coef_kernel, 7, [nd_shape] * 2)(*rest, wt, hb, hb_oth)
        got_nd = over("core", give)
        if not last:
            (nd,) = call(fold_kernel, 2, [((2 * RANK + TAIL, PAIR), i16)])(keep, got_nd)
            ht, hb = call(step_kernel, 3, [((RANK, PAIR), f32), ((RANK, PAIR), bf)])(
                nd, over("yhi", nd), ht
            )

    nd, nd_give = call(
        fold_last_kernel, 2, [((2, RANK, ROWS), f32), ((2 * RANK + TAIL, ROWS), i16)]
    )(keep, got_nd)
    (h_send,) = call(step_last_kernel, 3, [((N_WAVE, RANK + TAIL, ROWS), i16)])(
        nd, over("yhi", nd_give), ht
    )
    h_got = lax.all_to_all(h_send, WAVE, 0, 0, tiled=True)
    (coef,) = call(coef_out_kernel, 1, [((N_WAVE * ROWS, RANK), f32)])(h_got)

    mine = lax.dynamic_slice_in_dim(w_codes, (wave // 2) * N_WAVE, N_WAVE, 0)
    (temps,) = call(temps_out_kernel, 3, [((RANK, WIDTH), f32)], smem=1)(
        core[None], mine, over("core", mine)
    )
    return (temps, coef)


def solution(mesh):
    fine = Mesh(mesh.devices.reshape(2, 4, 2, 2, 2, 2), AXES)
    in_specs = (
        P(SPEC, WAVE),
        P(SPEC),
        P(SPEC),
        P(SPEC),
        P(SPEC, None),
        P(None, WAVE),
    )
    out_specs = (P(None, WAVE), P(SPEC, None))
    return jax.shard_map(shards, mesh=fine, in_specs=in_specs, out_specs=out_specs, check_vma=False)
```

time: 415 us -> 288 us (0.69)
  blocking collectives: 211 us -> 121 us
  Pallas kernels: 75.3 us -> 32.7 us
  local copies, waits for them, and re-layouts: 23.4 us -> 10.7 us
  starting transfers between devices: 19.2 us -> 30.3 us
  waiting for transfers between devices: 79.6 us -> 90.2 us
    all_to_all x3, blocking collectives: 108 us -> 60.5 us  [shards(): got_sums = lax.all_to_all(sums, CHIP, 0, 0, tiled=True)]
    pallas_call x13 -> x25, Pallas kernels: 75.3 us -> 32.7 us  [the longest x4 10.7 us: shards(): keep, give = call(coef_kernel, 7, [nd_shape] * 2)(*rest, wt, hb, hb_oth)]
    all_to_all x4, blocking collectives: 102 us -> 60.7 us  [shards(): wt = lax.all_to_all(send, CHIP, 0, 0, tiled=True)]
    ppermute x7 -> x17, waiting for transfers between devices: 7.11 us -> 38.3 us  [over(): return lax.ppermute(x, axis, [(0, 1), (1, 0)])]
    all_to_all x1, waiting for transfers between devices: 29 us -> 15.1 us  [shards(): got_sums = lax.all_to_all(sums, CHIP, 0, 0, tiled=True)]
    ppermute x7 -> x17, starting transfers between devices: 1.25 us -> 9.52 us  [over(): return lax.ppermute(x, axis, [(0, 1), (1, 0)])]
    unnamed x24 -> x9, local copies, waits for them, and re-layouts: 9.07 us -> 2.11 us
    all_to_all x2 -> x3, waiting for transfers between devices: 43.5 us -> 36.7 us  [the longest x1 23.5 us: shards(): got = lax.all_to_all(flux_t, WAVE, 0, 0, tiled=True)]
  transfers between devices with their start and end apart: 10 -> 21, of which waited for: 7 -> 18; matrix products, arithmetic and copies ran while one was open for 3% -> 2% of each run, Pallas kernels for 0% -> 1%
where the time goes in v2:
time: 288 us; the launch traced here: 287 us
  blocking collectives  121 us (42%)
  waiting for transfers between devices  90.2 us (31%)
  Pallas kernels  32.7 us (11%)
  starting transfers between devices  30.3 us (11%)
  local copies, waits for them, and re-layouts  10.7 us (4%)
    all_to_all x4, blocking collectives, shards(): wt = lax.all_to_all(send, CHIP, 0, 0, tiled=True)  60.7 us
    all_to_all x3, blocking collectives, shards(): got_sums = lax.all_to_all(sums, CHIP, 0, 0, tiled=True)  60.5 us
    ppermute x17, waiting for transfers between devices, over(): return lax.ppermute(x, axis, [(0, 1), (1, 0)])  38.3 us
    all_to_all x1, waiting for transfers between devices, shards(): got = lax.all_to_all(flux_t, WAVE, 0, 0, tiled=True)  23.5 us
    all_to_all x1, waiting for transfers between devices, shards(): got_sums = lax.all_to_all(sums, CHIP, 0, 0, tiled=True)  15.1 us
    pallas_call x4, Pallas kernels, shards(): keep, give = call(coef_kernel, 7, [nd_shape] * 2)(*rest, wt, hb, hb_oth)  10.7 us
    pallas_call x4, Pallas kernels, shards(): sums, = call(template_kernel, 7, [sums_shape], stats)(*rest, wt, hb, hb_oth)  10.6 us
    ppermute x17, starting transfers between devices, over(): return lax.ppermute(x, axis, [(0, 1), (1, 0)])  9.52 us
  transfers between devices with their start and end apart: 21, of which 18 were waited for; matrix products, arithmetic and copies ran while one was open for 2% of the time, Pallas kernels for 1%

profile of v2, /device:TPU:0, one launch (start us, length us, event | category | flops | bytes accessed | tf_op | source)
XLA Modules:
  0.0 286.8 jit_solution(1552702764184482511)
XLA Ops:
  0.6 3.8 %copy.12 = bf16[8,128,896]{1,2,0:T(8,128)(2,1)} copy(bf16[8,128,896]{2,1,0:T(8,128)(2,1)} %bitcast.68) | data formatting | bytes 3670016 | tf_op jit(solution)/shard_map/reshape | solution.py:273
  4.4 8.2 %all-to-all-start = ((bf16[8,896,128]{2,1,0:T(8,128)(2,1)}), bf16[8,896,128]{2,1,0:T(8,128)(2,1)S(1)}, u32[]{:S(2)}, u32[]{:S(2)}) async-start(bf16[8,896,128]{2,1,0:T(8,128)(2,1)} %bitcast.67), calls=%async_computation | async-start | bytes 3670016 | tf_op jit(solution)/shard_map/all_to_all | solution.py:274
  12.6 0.6 dynamic_slice.25
  13.2 0.7 pad_add_fusion.sc_ref
  13.9 0.8 dynamic-slice_bitcast_fusion.1
  14.7 23.5 %all-to-all-done.obs_ref = bf16[8,896,128]{2,1,0:T(8,128)(2,1)S(1)} async-done(((bf16[8,896,128]{2,1,0:T(8,128)(2,1)}), bf16[8,896,128]{2,1,0:T(8,128)(2,1)S(1)}, u32[]{:S(2)}, u32[]{:S(2)}) %all-to-all-start) | async-done | bytes 1835040 | tf_op jit(solution)/shard_map/all_to_all | solution.py:274
  38.2 2.8 shard_map.78
  41.0 1.0 copy.13
  42.0 0.8 collective-permute-start
  42.8 2.8 shard_map.77
  45.5 0.2 collective-permute-start.1
  45.8 2.7 collective-permute-start.3
  48.5 1.0 dynamic-slice_convert_fusion
  49.4 0.8 broadcast_in_dim.15
  50.3 3.5 %all-to-all-start.1 = ((bf16[4,448,128]{2,1,0:T(8,128)(2,1)}), bf16[4,448,128]{2,1,0:T(8,128)(2,1)S(1)}, u32[]{:S(2)}, u32[]{:S(2)}) async-start(bf16[4,448,128]{2,1,0:T(8,128)(2,1)} %broadcast_in_dim.15), calls=%async_computation.1 | async-start | bytes 917504 | tf_op jit(solution)/shard_map/all_to_all | solution.py:299
  53.8 0.9 constant_dynamic-slice_fusion.2
  55.0 1.2 collective-permute-done.4.hb_oth_ref
  56.2 6.7 %all-to-all-done.1 = bf16[4,448,128]{2,1,0:T(8,128)(2,1)S(1)} async-done(((bf16[4,448,128]{2,1,0:T(8,128)(2,1)}), bf16[4,448,128]{2,1,0:T(8,128)(2,1)S(1)}, u32[]{:S(2)}, u32[]{:S(2)}) %all-to-all-start.1) | async-done | bytes 458784 | tf_op jit(solution)/shard_map/all_to_all | solution.py:299
  62.9 3.3 %collective-permute-done.3 = bf16[32,56,128]{2,1,0:T(8,128)(2,1)S(1)} collective-permute-done((bf16[32,56,128]{2,1,0:T(8,128)(2,1)}, bf16[32,56,128]{2,1,0:T(8,128)(2,1)S(1)}, u32[]{:S(2)}, u32[]{:S(2)}) %collective-permute-start.3) | collective-permute-done | bytes 458784 | tf_op jit(solution)/shard_map/ppermute | solution.py:261
  66.2 2.6 shard_map.79
  68.9 1.0 copy-done
  69.8 5.7 %all-to-all-start.2 = ((s16[32,120,128]{2,1,0:T(8,128)(2,1)}), s16[32,120,128]{2,1,0:T(8,128)(2,1)S(1)}, u32[]{:S(2)}, u32[]{:S(2)}) async-start(s16[32,120,128]{2,1,0:T(8,128)(2,1)} %copy-done), calls=%async_computation.2 | async-start | bytes 1966080 | tf_op jit(solution)/shard_map/all_to_all | solution.py:314
  75.6 0.8 dynamic-slice_bitcast_fusion.w_ref
  76.3 15.1 %all-to-all-done.2.got_ref = s16[32,120,128]{2,1,0:T(8,128)(2,1)S(1)} async-done(((s16[32,120,128]{2,1,0:T(8,128)(2,1)}), s16[32,120,128]{2,1,0:T(8,128)(2,1)S(1)}, u32[]{:S(2)}, u32[]{:S(2)}) %all-to-all-start.2) | async-done | bytes 983072 | tf_op jit(solution)/shard_map/all_to_all | solution.py:314
  91.4 0.4 shard_map.80
  91.8 15.2 %all_to_all.55 = bf16[32,56,128]{2,1,0:T(8,128)(2,1)S(1)} all-to-all(bf16[32,56,128]{2,1,0:T(8,128)(2,1)S(1)} %get-tuple-element.35), channel_id=1, replica_groups=mesh['ylo'=2,'x'=4,'core'=2,'zh'=2,'zl'=2,'yhi'=2] {'zh','zl','ylo','x'}, dimensions={0} | all-to-all | bytes 917504 | tf_op jit(solution)/shard_map/all_to_all | solution.py:319
  107.0 2.7 shard_map.81
  109.8 1.5 collective-permute-done.5.b_ref
  111.4 1.2 collective-permute-start.6
  112.6 6.0 %collective-permute-done.6.oth_ref = s16[264,256]{1,0:T(8,128)(2,1)S(1)} collective-permute-done((s16[264,256]{1,0:T(8,128)(2,1)S(1)}, s16[264,256]{1,0:T(8,128)(2,1)S(1)}, u32[]{:S(2)}, u32[]{:S(2)}) %collective-permute-start.6) | collective-permute-done | bytes 135200 | tf_op jit(solution)/shard_map/ppermute | solution.py:261
  118.8 1.2 collective-permute-done.7.hb_oth_ref
  120.1 2.6 shard_map.84
  122.7 20.2 %all_to_all.56.got_ref = s16[32,120,128]{2,1,0:T(8,128)(2,1)S(1)} all-to-all(s16[32,120,128]{2,1,0:T(8,128)(2,1)S(1)} %shard_map.84), channel_id=1, replica_groups=mesh['ylo'=2,'x'=4,'core'=2,'zh'=2,'zl'=2,'yhi'=2] {'zh','zl','ylo','x'}, dimensions={0} | all-to-all | bytes 1966080 | tf_op jit(solution)/shard_map/all_to_all | solution.py:314
  142.9 0.4 shard_map.85
  143.3 15.0 %all_to_all.57 = bf16[32,56,128]{2,1,0:T(8,128)(2,1)S(1)} all-to-all(bf16[32,56,128]{2,1,0:T(8,128)(2,1)S(1)} %get-tuple-element.40), channel_id=1, replica_groups=mesh['ylo'=2,'x'=4,'core'=2,'zh'=2,'zl'=2,'yhi'=2] {'zh','zl','ylo','x'}, dimensions={0} | all-to-all | bytes 917504 | tf_op jit(solution)/shard_map/all_to_all | solution.py:319
  158.3 2.7 shard_map.86
  161.1 1.5 collective-permute-done.8.b_ref
  162.7 1.2 collective-permute-start.9
  163.9 6.0 %collective-permute-done.9.oth_ref = s16[264,256]{1,0:T(8,128)(2,1)S(1)} collective-permute-done((s16[264,256]{1,0:T(8,128)(2,1)S(1)}, s16[264,256]{1,0:T(8,128)(2,1)S(1)}, u32[]{:S(2)}, u32[]{:S(2)}) %collective-permute-start.9) | collective-permute-done | bytes 135200 | tf_op jit(solution)/shard_map/ppermute | solution.py:261
  170.1 1.2 collective-permute-done.10.hb_oth_ref
  171.4 2.7 shard_map.89
  174.0 20.2 %all_to_all.58.got_ref = s16[32,120,128]{2,1,0:T(8,128)(2,1)S(1)} all-to-all(s16[32,120,128]{2,1,0:T(8,128)(2,1)S(1)} %shard_map.89), channel_id=1, replica_groups=mesh['ylo'=2,'x'=4,'core'=2,'zh'=2,'zl'=2,'yhi'=2] {'zh','zl','ylo','x'}, dimensions={0} | all-to-all | bytes 1966080 | tf_op jit(solution)/shard_map/all_to_all | solution.py:314
  194.2 0.4 shard_map.90
  194.6 15.0 %all_to_all.59 = bf16[32,56,128]{2,1,0:T(8,128)(2,1)S(1)} all-to-all(bf16[32,56,128]{2,1,0:T(8,128)(2,1)S(1)} %get-tuple-element.46), channel_id=1, replica_groups=mesh['ylo'=2,'x'=4,'core'=2,'zh'=2,'zl'=2,'yhi'=2] {'zh','zl','ylo','x'}, dimensions={0} | all-to-all | bytes 917504 | tf_op jit(solution)/shard_map/all_to_all | solution.py:319
  209.6 2.7 shard_map.91
  212.3 1.5 collective-permute-done.11.b_ref
  214.0 1.4 collective-permute-start.12
  215.4 6.0 %collective-permute-done.12.oth_ref = s16[264,256]{1,0:T(8,128)(2,1)S(1)} collective-permute-done((s16[264,256]{1,0:T(8,128)(2,1)S(1)}, s16[264,256]{1,0:T(8,128)(2,1)S(1)}, u32[]{:S(2)}, u32[]{:S(2)}) %collective-permute-start.12) | collective-permute-done | bytes 135200 | tf_op jit(solution)/shard_map/ppermute | solution.py:261
  221.6 1.2 collective-permute-done.13.hb_oth_ref
  222.8 2.7 shard_map.94
  225.5 20.2 %all_to_all.60.got_ref = s16[32,120,128]{2,1,0:T(8,128)(2,1)S(1)} all-to-all(s16[32,120,128]{2,1,0:T(8,128)(2,1)S(1)} %shard_map.94), channel_id=1, replica_groups=mesh['ylo'=2,'x'=4,'core'=2,'zh'=2,'zl'=2,'yhi'=2] {'zh','zl','ylo','x'}, dimensions={0} | all-to-all | bytes 1966080 | tf_op jit(solution)/shard_map/all_to_all | solution.py:314
  245.6 1.0 shard_map.95
  246.6 15.6 %all_to_all.61.codes_ref = s16[32,64,128]{2,1,0:T(8,128)(2,1)S(1)} all-to-all(s16[32,64,128]{2,1,0:T(8,128)(2,1)S(1)} %get-tuple-element.52), channel_id=1, replica_groups=mesh['ylo'=2,'x'=4,'core'=2,'zh'=2,'zl'=2,'yhi'=2] {'zh','zl','ylo','x'}, dimensions={0} | all-to-all | bytes 1048576 | tf_op jit(solution)/shard_map/all_to_all | solution.py:319
  262.2 0.2 shard_map.97
  262.4 2.7 shard_map.98
  265.2 1.5 collective-permute-done.15.b_ref
  266.8 1.2 collective-permute-start.16
  268.0 4.7 %collective-permute-done.16.oth_ref = s16[264,128]{1,0:T(8,128)(2,1)S(1)} collective-permute-done((s16[264,128]{1,0:T(8,128)(2,1)S(1)}, s16[264,128]{1,0:T(8,128)(2,1)S(1)}, u32[]{:S(2)}, u32[]{:S(2)}) %collective-permute-start.16) | collective-permute-done | bytes 67616 | tf_op jit(solution)/shard_map/ppermute | solution.py:261
  272.6 0.8 shard_map.100
  273.5 3.4 %all-to-all-start.10 = ((s16[8,136,128]{2,1,0:T(8,128)(2,1)}), s16[8,136,128]{2,1,0:T(8,128)(2,1)S(1)}, u32[]{:S(2)}, u32[]{:S(2)}) async-start(s16[8,136,128]{2,1,0:T(8,128)(2,1)} %shard_map.100), calls=%async_computation.10 | async-start | bytes 557056 | tf_op jit(solution)/shard_map/all_to_all | solution.py:338
  277.0 1.3 collective-permute-done.14.theirs_ref
  278.3 1.0 shard_map.96
  279.3 6.4 %all-to-all-done.10.got_ref = s16[8,136,128]{2,1,0:T(8,128)(2,1)S(1)} async-done(((s16[8,136,128]{2,1,0:T(8,128)(2,1)}), s16[8,136,128]{2,1,0:T(8,128)(2,1)S(1)}, u32[]{:S(2)}, u32[]{:S(2)}) %all-to-all-start.10) | async-done | bytes 278560 | tf_op jit(solution)/shard_map/all_to_all | solution.py:338
  285.8 1.0 shard_map.101
  (30 shorter events, 1.8 us)
Async XLA Ops:
  4.4 8.2 %copy-start.2 = (s32[4]{0:T(128)S(1)}, s32[4]{0:T(128)}, u32[]{:S(2)}) copy-start(s32[4]{0:T(128)} %param.7) | copy-start | bytes 52
  4.4 33.8 %all-to-all-start = ((bf16[8,896,128]{2,1,0:T(8,128)(2,1)}), bf16[8,896,128]{2,1,0:T(8,128)(2,1)S(1)}, u32[]{:S(2)}, u32[]{:S(2)}) async-start(bf16[8,896,128]{2,1,0:T(8,128)(2,1)} %bitcast.67), calls=%async_computation | async-start | bytes 3670016 | tf_op jit(solution)/shard_map/all_to_all | solution.py:274
  12.5 28.4 %copy-start.1 = (f32[128,896]{1,0:T(8,128)S(1)}, f32[128,896]{1,0:T(8,128)}, u32[]{:S(2)}) copy-start(f32[128,896]{1,0:T(8,128)} %param.11) | copy-start | bytes 1376260
  41.0 4.8 %collective-permute-start.2 = (bf16[32,56,128]{2,1,0:T(8,128)(2,1)}, bf16[32,56,128]{2,1,0:T(8,128)(2,1)}, u32[]{:S(2)}, u32[]{:S(2)}) collective-permute-start(bf16[32,56,128]{2,1,0:T(8,128)(2,1)} %get-tuple-element.33), channel_id=1, source_target_pairs={{0,8},{8,0},{1,9},{9,1},{2,10},{10,2},{3,11},{11,3},{4,12},{12,4},... | collective-permute-start | bytes 1376264 | tf_op jit(solution)/shard_map/ppermute | solution.py:261
  42.0 21.0 %collective-permute-start = (bf16[32,56,128]{2,1,0:T(8,128)(2,1)S(1)}, bf16[32,56,128]{2,1,0:T(8,128)(2,1)S(1)}, u32[]{:S(2)}, u32[]{:S(2)}) collective-permute-start(bf16[32,56,128]{2,1,0:T(8,128)(2,1)S(1)} %get-tuple-element.31), channel_id=1, source_target_pairs={{0,1},{1,0},{2,3},{3,2},{4,5},{5,4},{6,7},{7,6},{8,9},{9,8},{10,11... | collective-permute-start | bytes 1376264 | tf_op jit(solution)/shard_map/ppermute | solution.py:261
  45.5 17.4 %collective-permute-start.1 = (bf16[32,56,128]{2,1,0:T(8,128)(2,1)}, bf16[32,56,128]{2,1,0:T(8,128)(2,1)S(1)}, u32[]{:S(2)}, u32[]{:S(2)}) collective-permute-start(bf16[32,56,128]{2,1,0:T(8,128)(2,1)} %get-tuple-element.32), channel_id=1, source_target_pairs={{0,8},{8,0},{1,9},{9,1},{2,10},{10,2},{3,11},{11,3},{4,12},{12,4},... | collective-permute-start | bytes 1376264 | tf_op jit(solution)/shard_map/ppermute | solution.py:261
  45.8 20.5 %collective-permute-start.3 = (bf16[32,56,128]{2,1,0:T(8,128)(2,1)}, bf16[32,56,128]{2,1,0:T(8,128)(2,1)S(1)}, u32[]{:S(2)}, u32[]{:S(2)}) collective-permute-start(bf16[32,56,128]{2,1,0:T(8,128)(2,1)} %collective-permute-done.2), channel_id=1, source_target_pairs={{0,1},{1,0},{2,3},{3,2},{4,5},{5,4},{6,7},{7,6},{8,9},{9,8},{10,11... | collective-permute-start | bytes 1376264 | tf_op jit(solution)/shard_map/ppermute | solution.py:261
  50.3 12.7 %all-to-all-start.1 = ((bf16[4,448,128]{2,1,0:T(8,128)(2,1)}), bf16[4,448,128]{2,1,0:T(8,128)(2,1)S(1)}, u32[]{:S(2)}, u32[]{:S(2)}) async-start(bf16[4,448,128]{2,1,0:T(8,128)(2,1)} %broadcast_in_dim.15), calls=%async_computation.1 | async-start | bytes 917504 | tf_op jit(solution)/shard_map/all_to_all | solution.py:299
  54.9 1.3 collective-permute-start.4
  68.9 1.0 copy-start
  69.8 21.6 %all-to-all-start.2 = ((s16[32,120,128]{2,1,0:T(8,128)(2,1)}), s16[32,120,128]{2,1,0:T(8,128)(2,1)S(1)}, u32[]{:S(2)}, u32[]{:S(2)}) async-start(s16[32,120,128]{2,1,0:T(8,128)(2,1)} %copy-done), calls=%async_computation.2 | async-start | bytes 1966080 | tf_op jit(solution)/shard_map/all_to_all | solution.py:314
  109.7 1.6 collective-permute-start.5
  111.4 7.2 %collective-permute-start.6 = (s16[264,256]{1,0:T(8,128)(2,1)S(1)}, s16[264,256]{1,0:T(8,128)(2,1)S(1)}, u32[]{:S(2)}, u32[]{:S(2)}) collective-permute-start(s16[264,256]{1,0:T(8,128)(2,1)S(1)} %shard_map.82.mine_ref), channel_id=1, source_target_pairs={{0,1},{1,0},{2,3},{3,2},{4,5},{5,4},{6,7},{7,6},{8,9},{9,8},{10,11... | collective-permute-start | bytes 405512 | tf_op jit(solution)/shard_map/ppermute | solution.py:261
  118.7 1.3 collective-permute-start.7
  161.0 1.6 collective-permute-start.8
  162.7 7.2 %collective-permute-start.9 = (s16[264,256]{1,0:T(8,128)(2,1)S(1)}, s16[264,256]{1,0:T(8,128)(2,1)S(1)}, u32[]{:S(2)}, u32[]{:S(2)}) collective-permute-start(s16[264,256]{1,0:T(8,128)(2,1)S(1)} %shard_map.87.mine_ref), channel_id=1, source_target_pairs={{0,1},{1,0},{2,3},{3,2},{4,5},{5,4},{6,7},{7,6},{8,9},{9,8},{10,11... | collective-permute-start | bytes 405512 | tf_op jit(solution)/shard_map/ppermute | solution.py:261
  170.0 1.3 collective-permute-start.10
  212.2 1.6 collective-permute-start.11
  214.0 7.4 %collective-permute-start.12 = (s16[264,256]{1,0:T(8,128)(2,1)S(1)}, s16[264,256]{1,0:T(8,128)(2,1)S(1)}, u32[]{:S(2)}, u32[]{:S(2)}) collective-permute-start(s16[264,256]{1,0:T(8,128)(2,1)S(1)} %shard_map.92.mine_ref), channel_id=1, source_target_pairs={{0,1},{1,0},{2,3},{3,2},{4,5},{5,4},{6,7},{7,6},{8,9},{9,8},{10,11... | collective-permute-start | bytes 405512 | tf_op jit(solution)/shard_map/ppermute | solution.py:261
  221.5 1.3 collective-permute-start.13
  265.1 1.6 collective-permute-start.15
  266.8 5.9 %collective-permute-start.16 = (s16[264,128]{1,0:T(8,128)(2,1)S(1)}, s16[264,128]{1,0:T(8,128)(2,1)S(1)}, u32[]{:S(2)}, u32[]{:S(2)}) collective-permute-start(s16[264,128]{1,0:T(8,128)(2,1)S(1)} %get-tuple-element.56), channel_id=1, source_target_pairs={{0,1},{1,0},{2,3},{3,2},{4,5},{5,4},{6,7},{7,6},{8,9},{9,8},{10,11... | collective-permute-start | bytes 202760 | tf_op jit(solution)/shard_map/ppermute | solution.py:261
  273.5 12.3 %all-to-all-start.10 = ((s16[8,136,128]{2,1,0:T(8,128)(2,1)}), s16[8,136,128]{2,1,0:T(8,128)(2,1)S(1)}, u32[]{:S(2)}, u32[]{:S(2)}) async-start(s16[8,136,128]{2,1,0:T(8,128)(2,1)} %shard_map.100), calls=%async_computation.10 | async-start | bytes 557056 | tf_op jit(solution)/shard_map/all_to_all | solution.py:338
  276.9 1.4 collective-permute-start.14
